TPU v7x, 512 devices: a whole 4x4x16 slice. The times are simulated.
512 devices in a mesh: replica: 8 (over z_lo), fsdp: 64 (over y, x, z_hi, core).
Axes of the slice: x: 4, y: 4, z: 16 (z_hi: 2, z_lo: 8; z = z_hi * 8 + z_lo), core: 2. Of those that a mesh axis runs over, the one named last changes fastest.
Arguments:
- tokens: bfloat16 [131072, 7168], P(('replica', 'fsdp')), may hold values from -24 to 24
- cotangent: bfloat16 [131072, 128], P(('replica', 'fsdp')), may hold values from -0.046875 to 0.046875
- keep_mask: int32 [131072], P(('replica', 'fsdp')), may hold values 0 or 1
- key_weight: bfloat16 [8, 7168, 128], P('replica', 'fsdp'), may hold values from -0.0625 to 0.0625
- norm_gain: float32 [8, 7168], P('replica', 'fsdp'), may hold values from 0.1 to 1.9
- local_params: float32 [8, 8, 262144], P('replica', None, 'fsdp'), may hold values from -1400 to 1400
- global_params: float32 [8, 262144], P(None, 'fsdp'), may hold values from -4 to 4
- momentum: float32 [8, 262144], P(None, 'fsdp'), may hold values from -6 to 6
- fragment_order: int32 [8], replicated, may hold values from 0 to 7, each once
Outputs:
- weight_grad: float32 [8, 7168, 128], P('replica', 'fsdp')
- gain_grad: float32 [8, 7168], P('replica', 'fsdp')
- local_out: float32 [8, 8, 262144], P('replica', None, 'fsdp')
- global_out: float32 [8, 262144], P(None, 'fsdp')
- moment_out: float32 [8, 262144], P(None, 'fsdp')
Inputs may be any that keep to these rules, and one draw needn't show every extreme that they name: `fragment_order`: its first 2 entries name the fragment's layers.
All inputs are finite; a program needn't handle non-finite values. No bound on the sum of `keep_mask` on one device may be relied on, other than what follows from the above.
Results may differ from a plain program's by a relative error of at most 0.005.
Values may be sent and summed in bfloat16 or wider, within the bound.
A program may use at most 64 MiB of HBM per device.

v0:
```python
import jax
import jax.numpy as jnp
from jax import lax
from jax.sharding import PartitionSpec as P

FRAG = 2


EPSILON = 1e-06
CLIP_RATE = 0.5
MOMENT = 0.9
OUTER_RATE = 0.7
MIX_RATE = 0.5


def outer_step(averaged, glob_rows, moment_rows, squares, count):
    limit = CLIP_RATE * jnp.sqrt(jnp.float32(count))
    factor = jnp.minimum(1.0, limit / jnp.sqrt(squares + EPSILON))
    clipped = averaged * factor
    moment_new = MOMENT * moment_rows + clipped
    global_new = glob_rows - OUTER_RATE * (clipped + MOMENT * moment_new)
    return (moment_new, global_new)


def inner_part(tokens, cotangent, keep_mask, key_weight, norm_gain):
    as_float = tokens.astype(jnp.float32)
    inv_rms = lax.rsqrt(jnp.mean(as_float * as_float, axis=1, keepdims=True) + EPSILON)
    unit_rows = as_float * inv_rms
    normed = unit_rows.astype(jnp.bfloat16)
    masked = jnp.where(keep_mask[:, None] == 1, cotangent, jnp.zeros_like(cotangent))
    hidden_grad = jnp.einsum(
        "th,dh->td",
        masked,
        lax.all_gather(key_weight[0], "fsdp", axis=0, tiled=True),
        preferred_element_type=jnp.float32,
    )
    gain_partial = jnp.sum(hidden_grad * unit_rows, axis=0)
    partial_grad = jnp.einsum("td,th->dh", normed, masked, preferred_element_type=jnp.float32)
    own_grad, gain_grad = (
        lax.psum_scatter(partial_grad, "fsdp", scatter_dimension=0, tiled=True),
        lax.psum_scatter(gain_partial, "fsdp", scatter_dimension=0, tiled=True),
    )
    weight_grad = (norm_gain[0][:, None] * own_grad)[None]
    return (weight_grad, gain_grad[None])


def outer_part(local_params, global_params, momentum, fragment_order):
    frag_rows = fragment_order[:FRAG]
    own_local = local_params[0]
    local_rows = jnp.take(own_local, frag_rows, axis=0)
    glob_rows = jnp.take(global_params, frag_rows, axis=0)
    moment_rows = jnp.take(momentum, frag_rows, axis=0)
    delta = glob_rows - local_rows
    replicas = lax.axis_size("replica")
    count = FRAG * global_params.shape[1] * lax.axis_size("fsdp")
    averaged = lax.psum(delta.astype(jnp.bfloat16), "replica").astype(jnp.float32) / replicas
    squares = lax.psum(jnp.sum(averaged * averaged), "fsdp")
    moment_new, global_new = outer_step(averaged, glob_rows, moment_rows, squares, count)
    merged = MIX_RATE * local_rows + (1.0 - MIX_RATE) * global_new
    local_out = own_local.at[frag_rows].set(merged)[None]
    global_out = global_params.at[frag_rows].set(global_new)
    moment_out = momentum.at[frag_rows].set(moment_new)
    return (local_out, global_out, moment_out)


def per_device(
    tokens,
    cotangent,
    keep_mask,
    key_weight,
    norm_gain,
    local_params,
    global_params,
    momentum,
    fragment_order,
):
    weight_grad, gain_grad = inner_part(tokens, cotangent, keep_mask, key_weight, norm_gain)
    local_out, global_out, moment_out = outer_part(
        local_params, global_params, momentum, fragment_order
    )
    return (weight_grad, gain_grad, local_out, global_out, moment_out)


def solution(mesh):
    in_specs = (
        P(("replica", "fsdp"), None),
        P(("replica", "fsdp"), None),
        P(("replica", "fsdp")),
        P("replica", "fsdp", None),
        P("replica", "fsdp"),
        P("replica", None, "fsdp"),
        P(None, "fsdp"),
        P(None, "fsdp"),
        P(),
    )
    out_specs = (
        P("replica", "fsdp", None),
        P("replica", "fsdp"),
        P("replica", None, "fsdp"),
        P(None, "fsdp"),
        P(None, "fsdp"),
    )
    return jax.shard_map(
        per_device, mesh=mesh, in_specs=in_specs, out_specs=out_specs, check_vma=False
    )
```

profile of v0, /device:TPU:1, one launch (start us, length us, event | category | flops | bytes accessed | tf_op | source)
XLA Modules:
  0.0 698.6 jit_solution(16205948114486822126)
XLA Ops:
  7.2 0.0 copy-start.4
  7.2 0.0 all-gather.3.cloned.1.call-start
  7.2 0.9 copy.20
  8.1 0.9 copy.21
  9.0 0.9 copy.22
  9.9 0.0 all-gather.3.cloned.1.call-update
  10.0 0.0 reduce-scatter.2.cloned.1.call-start
  10.0 0.0 copy-start
  10.0 0.8 broadcast_compare_fusion
  10.9 3.0 fusion.1
  13.9 0.0 copy-done.4
  13.9 0.0 copy-done
  13.9 3.3 fusion.2
  17.2 0.0 copy-start.6
  17.2 0.0 reduce-scatter.2.cloned.1.call-update
  17.2 0.6 copy-done.6
  17.9 0.6 gather_fusion
  18.4 0.6 gather_fusion.1
  19.0 0.6 gather_fusion.2
  19.6 1.3 dynamic-slice
  21.5 0.1 subtract_convert_fusion
  21.6 54.4 %psum.14 = bf16[2,4096]{1,0:T(2,128)(2,1)S(1)} all-reduce(bf16[2,4096]{1,0:T(2,128)(2,1)S(1)} %subtract_convert_fusion), channel_id=1, replica_groups=mesh['replica'=8,'fsdp'=64] {'replica'}, use_global_device_ids=true, to_apply=%region_4.6 | all-reduce | flops 8192 | bytes 32768 | tf_op jit(solution)/shard_map/psum | solution.py:56
  76.0 0.6 fusion.12
  76.7 0.0 copy-start.5
  76.7 52.4 %all-gather.3.cloned.1.call-done = bf16[1,7168,128]{2,1,0:T(8,128)(2,1)} async-done(((bf16[1,112,128]{2,1,0:T(8,128)(2,1)}), bf16[1,7168,128]{2,1,0:T(8,128)(2,1)}) %all-gather.3.cloned.1.call-update) | async-done | bytes 1835024 | tf_op jit(solution)/shard_map/all_gather | solution.py:34
  129.1 3.8 fusion.5
  132.9 542.6 %all-reduce.1 = (f32[7168]{0:T(1024)S(1)}, f32[]{:T(128)}) all-reduce(f32[7168]{0:T(1024)S(1)} %fusion.5, f32[]{:T(128)} %fusion.12), channel_id=4, replica_groups=mesh['replica'=8,'fsdp'=64] {'fsdp'}, use_global_device_ids=true, to_apply=%region_3.4.clone | all-reduce | flops 7169 | bytes 57352
  676.2 0.8 scatter_custom_fusion.1
  677.0 0.0 copy-start.3
  677.0 0.8 scatter_custom_fusion.2
  677.8 0.0 copy-start.2
  677.8 0.8 scatter_custom_fusion
  678.7 0.0 copy-start.1
  678.7 0.6 dynamic-slice_bitcast_fusion
  679.3 10.9 %reduce-scatter.2.cloned.1.call-done = f32[112,128]{1,0:T(8,128)} async-done(((f32[7168,128]{1,0:T(8,128)}), f32[112,128]{1,0:T(8,128)}) %reduce-scatter.2.cloned.1.call-update) | async-done | bytes 57360 | tf_op jit(solution)/shard_map/reduce_scatter | solution.py:40
  690.2 0.0 copy-done.5
  690.2 1.5 multiply_bitcast_fusion
  691.7 0.0 copy-done.3
  691.7 0.0 copy-done.2
  691.7 0.0 copy-done.1
  (3 shorter events, 0.0 us)
Async XLA Ops:
  7.2 6.7 copy-start.4
  7.2 121.9 %all-gather.3.cloned.1.call-start = ((), (), s32[]{:S(2)}) async-start(), calls=%async_computation.2 | async-start | bytes 1863680 | tf_op jit(solution)/shard_map/all_gather | solution.py:34
  10.0 680.2 %reduce-scatter.2.cloned.1.call-start = ((), (), s32[]{:S(2)}) async-start(), calls=%async_computation.1 | async-start | bytes 3727360 | tf_op jit(solution)/shard_map/reduce_scatter | solution.py:40
  10.0 3.9 copy-start
  17.2 0.7 copy-start.6
  76.7 613.5 %copy-start.5 = (f32[1,112]{1,0:T(1,128)S(1)}, f32[1,112]{1,0:T(1,128)}, u32[]{:S(2)}) copy-start(f32[1,112]{1,0:T(1,128)} %param.15) | copy-start | bytes 1348
  677.0 14.7 %copy-start.3 = (f32[8,4096]{1,0:T(8,128)}, f32[8,4096]{1,0:T(8,128)S(1)}, u32[]{:S(2)}) copy-start(f32[8,4096]{1,0:T(8,128)S(1)} %scatter_custom_fusion.1) | copy-start | bytes 393220
  677.8 13.9 %copy-start.2 = (f32[8,4096]{1,0:T(8,128)}, f32[8,4096]{1,0:T(8,128)S(1)}, u32[]{:S(2)}) copy-start(f32[8,4096]{1,0:T(8,128)S(1)} %scatter_custom_fusion.2) | copy-start | bytes 393220
  678.7 13.1 %copy-start.1 = (f32[8,4096]{1,0:T(8,128)}, f32[8,4096]{1,0:T(8,128)S(1)}, u32[]{:S(2)}) copy-start(f32[8,4096]{1,0:T(8,128)S(1)} %scatter_custom_fusion) | copy-start | bytes 393220
Sparse Core Ops, SparseCore 0:
  12.5 116.5 all-gather.2
  131.9 558.2 reduce-scatter.1
where the time goes:
time: 711 us; the launch traced here: 699 us
  blocking collectives  597 us (84%)
  waiting for transfers between devices  63.3 us (9%)
  between operations  15.5 us (2%)
  other arithmetic  8.57 us (1%)
    unnamed x1, blocking collectives  543 us
    psum x1, blocking collectives, outer_part(): lax.psum(delta.astype(jnp.bfloat16), 'replica').astype(jnp.float32)  54.4 us
    all_gather x1, waiting for transfers between devices, inner_part(): lax.all_gather(key_weight[0], 'fsdp', axis=0, tiled=True)  52.4 us
  transfers between devices with their start and end apart: 2, of which 2 were waited for; matrix products, arithmetic and copies ran while one was open for 3% of the time, Pallas kernels for 0%

commit v1 on v0

v1 whole, which is shorter than its diff:
```python
import functools

import jax
import jax.numpy as jnp
from jax import lax
from jax.experimental import pallas as pl
from jax.experimental.pallas import tpu as pltpu
from jax.sharding import PartitionSpec as P

FRAG = 2

EPSILON = 1e-06
CLIP_RATE = 0.5
MOMENT = 0.9
OUTER_RATE = 0.7
MIX_RATE = 0.5

NY, NX, NZ, NC = 4, 4, 2, 2
LANES = 128
TOKEN_BLOCK = 32
MESH = pl.DeviceIdType.MESH


def far_first(count):
    return sorted(range(count), key=lambda off: (-min(off, count - off), off))


def exchange_kernel(
    replicas,
    tok_hbm,
    cot_ref,
    mask_ref,
    loc_hbm,
    glob_hbm,
    order_ref,
    sum_ref,
    avg_ref,
    sq_ref,
    tok,
    loc,
    glob,
    masked,
    part,
    core_out,
    core_in,
    x1_out,
    x1_in,
    y1_out,
    y1_in,
    x2_out,
    x2_in,
    y2_out,
    y2_in,
    z_out,
    z_in,
    delta,
    delta_in,
    sq_out,
    sq_in,
    tok_sem,
    par_sem,
    core_sem,
    x1_sem,
    y1_sem,
    x2_sem,
    y2_sem,
    z_sem,
    rs_sem,
    ag_sem,
    sq_sem,
):
    rep = lax.axis_index("replica")
    me = lax.axis_index("fsdp")
    core = lax.rem(me, NC)
    z = lax.rem(me // NC, NZ)
    x = lax.rem(me // (NC * NZ), NX)
    y = me // (NC * NZ * NX)

    def device(yy, xx, zz, cc):
        return (rep, ((yy * NX + xx) * NZ + zz) * NC + cc)

    def x_peer(off):
        return device(y, lax.rem(x + off, NX), z, core)

    def y_peer(off):
        return device(lax.rem(y + off, NY), x, z, core)

    def rep_peer(off):
        return (lax.rem(rep + off, replicas), me)

    core_peer = device(y, x, z, 1 - core)
    z_peer = device(y, x, 1 - z, core)

    tokens, width = tok.shape
    rows = part.shape[0] // (NY * NX * NZ * NC)
    chunk = width // NY
    offs = far_first(NY)
    own = offs.index(0)

    token_copies = [
        pltpu.make_async_copy(
            tok_hbm.at[pl.ds(i * TOKEN_BLOCK, TOKEN_BLOCK)],
            tok.at[pl.ds(i * TOKEN_BLOCK, TOKEN_BLOCK)],
            tok_sem.at[i],
        )
        for i in range(tokens // TOKEN_BLOCK)
    ]
    for copy in token_copies:
        copy.start()
    loc_copy = pltpu.make_async_copy(loc_hbm.at[0], loc, par_sem.at[0])
    glob_copy = pltpu.make_async_copy(glob_hbm, glob, par_sem.at[1])
    loc_copy.start()
    glob_copy.start()

    barrier = pltpu.get_barrier_semaphore()
    peers = [core_peer, z_peer]
    peers += [x_peer(off) for off in range(1, NX)]
    peers += [y_peer(off) for off in range(1, NY)]
    peers += [rep_peer(off) for off in range(1, replicas)]
    for peer in peers:
        pl.semaphore_signal(barrier, inc=1, device_id=peer, device_id_type=MESH)

    cot_t = cot_ref[...].astype(jnp.float32).T
    keep = jnp.broadcast_to(mask_ref[...] == 1, cot_t.shape)
    masked[...] = jnp.where(keep, cot_t, 0.0).astype(jnp.bfloat16)

    for i, copy in enumerate(token_copies):
        copy.wait()
        for half in range(TOKEN_BLOCK // 16):
            at = pl.ds(i * TOKEN_BLOCK + half * 16, 16)
            sums = [jnp.zeros((16, LANES), jnp.float32) for _ in range(4)]
            for j in range(width // LANES):
                piece = tok[at, j * LANES : (j + 1) * LANES].astype(jnp.float32)
                sums[j % 4] += piece * piece
            total = jnp.sum((sums[0] + sums[1]) + (sums[2] + sums[3]), axis=1, keepdims=True)
            inv_rms = lax.rsqrt(total / width + EPSILON)
            for j in range(width // LANES):
                piece = tok[at, j * LANES : (j + 1) * LANES].astype(jnp.float32)
                tok[at, j * LANES : (j + 1) * LANES] = (piece * inv_rms).astype(jnp.bfloat16)

    loc_copy.wait()
    glob_copy.wait()
    per_row = loc.shape[1] // LANES
    for i in range(FRAG):
        layer = order_ref[i]
        diff = glob[pl.ds(layer, 1), :] - loc[pl.ds(layer, 1), :]
        for j in range(per_row):
            delta[i * per_row + j : i * per_row + j + 1, :] = diff[:, j * LANES : (j + 1) * LANES]

    pl.semaphore_wait(barrier, len(peers))

    sent = []

    def send(src, dst, sems, index, peer):
        copy = pltpu.make_async_remote_copy(
            src_ref=src,
            dst_ref=dst,
            send_sem=sems.at[0, index],
            recv_sem=sems.at[1, index],
            device_id=peer,
            device_id_type=MESH,
        )
        copy.start()
        sent.append(copy)
        return copy

    shard = delta.shape[0] // replicas
    rs = [
        send(
            delta.at[pl.ds(pl.multiple_of(lax.rem(rep + off, replicas) * shard, 8), shard)],
            delta_in.at[off - 1],
            rs_sem,
            off - 1,
            rep_peer(off),
        )
        for off in range(1, replicas)
    ]

    def outer_reduce():
        for copy in rs:
            copy.wait_recv()
        mine = pl.ds(pl.multiple_of(rep * shard, 8), shard)
        total = delta[mine, :]
        for off in range(1, replicas):
            total = total + delta_in[off - 1]
        avg_ref[mine, :] = total / replicas
        return [
            send(avg_ref.at[mine], avg_ref.at[mine], ag_sem, off - 1, rep_peer(off))
            for off in range(1, replicas)
        ]

    def square_round(at, base, value, targets):
        sq_out[at] = value
        return [
            send(sq_out.at[at], sq_in.at[base + i], sq_sem, base + i, peer)
            for i, peer in enumerate(targets)
        ]

    def square_sum(at, base, copies):
        total = sq_out[at]
        for i, copy in enumerate(copies):
            copy.wait_recv()
            total = total + sq_in[base + i]
        return total

    def column(off):
        return lax.rem(y + off, NY)

    def block_at(yy, xx, zz, cc):
        start = (((yy * NX + xx) * NZ + zz) * NC + cc) * rows
        return pl.ds(pl.multiple_of(start, 16), rows)

    def multiply(k):
        yy = column(offs[k])
        done = 0
        while done < chunk:
            size = min(256, chunk - done)
            at = pl.multiple_of(yy * chunk + done, LANES)
            product = jnp.dot(
                masked[...], tok[:, pl.ds(at, size)], preferred_element_type=jnp.float32
            )
            part[pl.ds(at, size), :] = product.T
            done += size
        for xx in range(NX):
            for zz in range(NZ):
                core_out[k, xx * NZ + zz] = part[block_at(yy, xx, zz, 1 - core), :].astype(
                    jnp.bfloat16
                )
        return send(core_out.at[k], core_in.at[k], core_sem, k, core_peer)

    def chip_sum(k, xx, zz):
        mine = part[block_at(column(offs[k]), xx, zz, core), :]
        return mine + core_in[k, xx * NZ + zz].astype(jnp.float32)

    x1, y1 = {}, {}

    def spread(k):
        core_copies[k].wait_recv()
        for off in far_first(NX)[:-1]:
            slot = k * (NX - 1) + off - 1
            x1_out[slot] = chip_sum(k, lax.rem(x + off, NX), 0).astype(jnp.bfloat16)
            x1[slot] = send(x1_out.at[slot], x1_in.at[slot], x1_sem, slot, x_peer(off))
        if k != own:
            slot = offs[k] - 1
            for xx in range(NX):
                y1_out[slot, xx] = chip_sum(k, xx, 1).astype(jnp.bfloat16)
            y1[slot] = send(y1_out.at[slot], y1_in.at[slot], y1_sem, slot, y_peer(offs[k]))

    def x_sum(k):
        total = chip_sum(k, x, 0)
        for off in range(1, NX):
            slot = k * (NX - 1) + off - 1
            x1[slot].wait_recv()
            total = total + x1_in[slot].astype(jnp.float32)
        return total

    def y_sum(xx):
        total = chip_sum(own, xx, 1)
        for off in range(1, NY):
            total = total + y1_in[off - 1, xx].astype(jnp.float32)
        return total

    x2, y2 = {}, {}

    def forward_x(k):
        slot = offs[k] - 1
        x2_out[slot] = x_sum(k).astype(jnp.bfloat16)
        x2[slot] = send(x2_out.at[slot], x2_in.at[slot], x2_sem, slot, y_peer(offs[k]))

    def forward_y():
        for off in range(1, NY):
            y1[off - 1].wait_recv()
        for off in far_first(NX)[:-1]:
            y2_out[off - 1] = y_sum(lax.rem(x + off, NX)).astype(jnp.bfloat16)
            y2[off - 1] = send(
                y2_out.at[off - 1], y2_in.at[off - 1], y2_sem, off - 1, x_peer(off)
            )

    core_copies = {}
    core_copies[0] = multiply(0)
    core_copies[1] = multiply(1)
    ag = outer_reduce()
    spread(0)
    y_squares = []

    def outer_gather():
        for copy in ag:
            copy.wait_recv()
        squared = avg_ref[...] * avg_ref[...]
        folded = squared[0:8]
        for i in range(1, squared.shape[0] // 8):
            folded = folded + squared[i * 8 : (i + 1) * 8]
        y_squares.extend(square_round(0, 0, folded, [y_peer(off) for off in range(1, NY)]))

    for k in range(2, NY):
        core_copies[k] = multiply(k)
        spread(k - 1)
        if k == 2:
            outer_gather()
    if not y_squares:
        outer_gather()
    x_squares = square_round(
        1, NY - 1, square_sum(0, 0, y_squares), [x_peer(off) for off in range(1, NX)]
    )
    spread(NY - 1)
    for k in range(NY - 1):
        forward_x(k)
    forward_y()
    base = NY + NX - 2
    core_squares = square_round(2, base, square_sum(1, NY - 1, x_squares), [core_peer])
    first = x_sum(own)
    for off in range(1, NY):
        x2[off - 1].wait_recv()
        first = first + x2_in[off - 1].astype(jnp.float32)
    second = y_sum(x)
    for off in range(1, NX):
        y2[off - 1].wait_recv()
        second = second + y2_in[off - 1].astype(jnp.float32)
    z_out[...] = jnp.where(z == 0, second, first).astype(jnp.bfloat16)
    z_copy = send(z_out, z_in, z_sem, 0, z_peer)
    sum_ref[...] = jnp.where(z == 0, first, second)
    z_squares = square_round(3, base + 1, square_sum(2, base, core_squares), [z_peer])
    sq_ref[...] = square_sum(3, base + 1, z_squares)
    z_copy.wait_recv()
    sum_ref[...] = sum_ref[...] + z_in[...].astype(jnp.float32)
    for copy in sent:
        copy.wait_send()


def exchange(tokens, cotangent, keep_mask, local_params, global_params, order, rows, replicas):
    count, width = tokens.shape
    heads = cotangent.shape[1]
    held, params = global_params.shape
    lines = FRAG * params // LANES
    squares = NY + NX
    vmem = pl.BlockSpec(memory_space=pltpu.VMEM)
    hbm = pl.BlockSpec(memory_space=pl.ANY)
    bf16, f32 = jnp.bfloat16, jnp.float32
    block = (rows, heads)
    return pl.pallas_call(
        functools.partial(exchange_kernel, replicas),
        out_shape=(
            jax.ShapeDtypeStruct(block, f32),
            jax.ShapeDtypeStruct((lines, LANES), f32),
            jax.ShapeDtypeStruct((8, LANES), f32),
        ),
        in_specs=[hbm, vmem, vmem, hbm, hbm, pl.BlockSpec(memory_space=pltpu.SMEM)],
        out_specs=(vmem, vmem, vmem),
        scratch_shapes=[
            pltpu.VMEM((count, width), bf16),
            pltpu.VMEM((held, params), f32),
            pltpu.VMEM((held, params), f32),
            pltpu.VMEM((heads, count), bf16),
            pltpu.VMEM((width, heads), f32),
            pltpu.VMEM((NY, NX * NZ) + block, bf16),
            pltpu.VMEM((NY, NX * NZ) + block, bf16),
            pltpu.VMEM((NY * (NX - 1),) + block, bf16),
            pltpu.VMEM((NY * (NX - 1),) + block, bf16),
            pltpu.VMEM((NY - 1, NX) + block, bf16),
            pltpu.VMEM((NY - 1, NX) + block, bf16),
            pltpu.VMEM((NY - 1,) + block, bf16),
            pltpu.VMEM((NY - 1,) + block, bf16),
            pltpu.VMEM((NX - 1,) + block, bf16),
            pltpu.VMEM((NX - 1,) + block, bf16),
            pltpu.VMEM(block, bf16),
            pltpu.VMEM(block, bf16),
            pltpu.VMEM((lines, LANES), f32),
            pltpu.VMEM((replicas - 1, lines // replicas, LANES), f32),
            pltpu.VMEM((4, 8, LANES), f32),
            pltpu.VMEM((squares, 8, LANES), f32),
            pltpu.SemaphoreType.DMA((count // TOKEN_BLOCK,)),
            pltpu.SemaphoreType.DMA((2,)),
            pltpu.SemaphoreType.DMA((2, NY)),
            pltpu.SemaphoreType.DMA((2, NY * (NX - 1))),
            pltpu.SemaphoreType.DMA((2, NY - 1)),
            pltpu.SemaphoreType.DMA((2, NY - 1)),
            pltpu.SemaphoreType.DMA((2, NX - 1)),
            pltpu.SemaphoreType.DMA((2, 1)),
            pltpu.SemaphoreType.DMA((2, replicas - 1)),
            pltpu.SemaphoreType.DMA((2, replicas - 1)),
            pltpu.SemaphoreType.DMA((2, squares)),
        ],
        compiler_params=pltpu.CompilerParams(
            collective_id=0, has_side_effects=True, vmem_limit_bytes=32 * 1024 * 1024
        ),
        cost_estimate=pl.CostEstimate(
            flops=2 * count * width * heads, bytes_accessed=2 * count * width, transcendentals=0
        ),
    )(tokens, cotangent, keep_mask.reshape(1, count), local_params, global_params, order)


def finish_kernel(
    count,
    order_ref,
    sum_ref,
    avg_ref,
    sq_ref,
    weight_ref,
    gain_ref,
    loc_ref,
    glob_ref,
    mom_ref,
    weight_out,
    gain_out,
    loc_out,
    glob_out,
    mom_out,
):
    total = sum_ref[...]
    rows, heads = total.shape
    scale = jnp.broadcast_to(gain_ref[...], (heads, rows)).T
    weight_out[0] = scale * total
    product = weight_ref[0].astype(jnp.float32) * total
    gain_out[...] = jnp.sum(product.T, axis=0, keepdims=True)

    squares = jnp.sum(sq_ref[...])
    limit = CLIP_RATE * jnp.sqrt(jnp.float32(count))
    factor = jnp.minimum(1.0, limit / jnp.sqrt(jnp.full((8, LANES), squares) + EPSILON))
    held, params = glob_ref.shape
    layer = lax.broadcasted_iota(jnp.int32, (held, LANES), 0)
    first = layer == order_ref[0]
    second = layer == order_ref[1]
    picked = first | second
    lines = params // LANES
    for j in range(lines):
        at = slice(j * LANES, (j + 1) * LANES)
        averaged = jnp.where(
            first,
            jnp.broadcast_to(avg_ref[j : j + 1, :], (held, LANES)),
            jnp.broadcast_to(avg_ref[lines + j : lines + j + 1, :], (held, LANES)),
        )
        loc, glob, mom = loc_ref[0, :, at], glob_ref[:, at], mom_ref[:, at]
        clipped = averaged * factor
        moment_new = MOMENT * mom + clipped
        global_new = glob - OUTER_RATE * (clipped + MOMENT * moment_new)
        merged = MIX_RATE * loc + (1.0 - MIX_RATE) * global_new
        loc_out[0, :, at] = jnp.where(picked, merged, loc)
        glob_out[:, at] = jnp.where(picked, global_new, glob)
        mom_out[:, at] = jnp.where(picked, moment_new, mom)


def finish(order, total, averaged, squares, weight, gain, local_params, global_params, momentum, count):
    vmem = pl.BlockSpec(memory_space=pltpu.VMEM)
    shapes = (
        jax.ShapeDtypeStruct(weight.shape, jnp.float32),
        jax.ShapeDtypeStruct(gain.shape, jnp.float32),
        jax.ShapeDtypeStruct(local_params.shape, jnp.float32),
        jax.ShapeDtypeStruct(global_params.shape, jnp.float32),
        jax.ShapeDtypeStruct(momentum.shape, jnp.float32),
    )
    return pl.pallas_call(
        functools.partial(finish_kernel, count),
        out_shape=shapes,
        in_specs=[pl.BlockSpec(memory_space=pltpu.SMEM)] + [vmem] * 8,
        out_specs=(vmem,) * 5,
        compiler_params=pltpu.CompilerParams(vmem_limit_bytes=16 * 1024 * 1024),
    )(order, total, averaged, squares, weight, gain, local_params, global_params, momentum)


def per_device(
    replicas,
    fsdp,
    tokens,
    cotangent,
    keep_mask,
    key_weight,
    norm_gain,
    local_params,
    global_params,
    momentum,
    fragment_order,
):
    total, averaged, squares = exchange(
        tokens,
        cotangent,
        keep_mask,
        local_params,
        global_params,
        fragment_order,
        key_weight.shape[1],
        replicas,
    )
    count = FRAG * global_params.shape[1] * fsdp
    return finish(
        fragment_order,
        total,
        averaged,
        squares,
        key_weight,
        norm_gain,
        local_params,
        global_params,
        momentum,
        count,
    )


def solution(mesh):
    in_specs = (
        P(("replica", "fsdp"), None),
        P(("replica", "fsdp"), None),
        P(("replica", "fsdp")),
        P("replica", "fsdp", None),
        P("replica", "fsdp"),
        P("replica", None, "fsdp"),
        P(None, "fsdp"),
        P(None, "fsdp"),
        P(),
    )
    out_specs = (
        P("replica", "fsdp", None),
        P("replica", "fsdp"),
        P("replica", None, "fsdp"),
        P(None, "fsdp"),
        P(None, "fsdp"),
    )
    return jax.shard_map(
        functools.partial(per_device, mesh.shape["replica"], mesh.shape["fsdp"]),
        mesh=mesh,
        in_specs=in_specs,
        out_specs=out_specs,
        check_vma=False,
    )
```

time: 711 us -> 55.5 us (0.08); the launches traced: 699 us -> 55.3 us
  blocking collectives: 597 us -> 0 us
  waiting for transfers between devices: 63.3 us -> 0 us
  Pallas kernels: 0 us -> 48.5 us
  between operations: 15.5 us -> 0.69 us
  other arithmetic: 8.57 us -> 0 us
    unnamed x1 -> x0, blocking collectives: 543 us -> none
    psum x1 -> x0, blocking collectives: 54.4 us -> none  [outer_part(): lax.psum(delta.astype(jnp.bfloat16), 'replica').astype(jnp.float32)]
    all_gather x1 -> x0, waiting for transfers between devices: 52.4 us -> none  [inner_part(): lax.all_gather(key_weight[0], 'fsdp', axis=0, tiled=True)]
    pallas_call x0 -> x2, Pallas kernels: none -> 48.5 us  [the longest x1 47.1 us: exchange(): pl.pallas_call(functools.partial(exchange_kernel, replicas), out_shape=(j...]
    reduce_scatter x1 -> x0, waiting for transfers between devices: 10.9 us -> none  [inner_part(): lax.psum_scatter(partial_grad, 'fsdp', scatter_dimension=0, tiled=True)]
  transfers between devices with their start and end apart: 2 -> 0, of which waited for: 2 -> 0; matrix products, arithmetic and copies ran while one was open for 3% -> 0% of each run, Pallas kernels for 0% -> 0%
where the time goes in v1:
time: 55.5 us; the launch traced here: 55.3 us
  Pallas kernels  48.5 us (87%)
  local copies, waits for them, and re-layouts  6.03 us (11%)
  between operations  0.69 us (1%)
    pallas_call x1, Pallas kernels, exchange(): pl.pallas_call(functools.partial(exchange_kernel, replicas), out_shape=(j...  47.1 us
    unnamed x18, local copies, waits for them, and re-layouts  6.03 us
    pallas_call x1, Pallas kernels, finish(): pl.pallas_call(functools.partial(finish_kernel, count), out_shape=shapes,...  1.49 us

profile of v1, /device:TPU:1, one launch (start us, length us, event | category | flops | bytes accessed | tf_op | source)
XLA Modules:
  0.0 55.3 jit_solution(8899537856994474670)
XLA Ops:
  0.6 0.0 copy-start.8
  0.6 0.0 copy-start
  0.7 2.0 %copy-done = bf16[256,7168]{1,0:T(8,128)(2,1)S(1)} copy-done((bf16[256,7168]{1,0:T(8,128)(2,1)S(1)}, bf16[256,7168]{1,0:T(8,128)(2,1)}, u32[]{:S(2)}) %copy-start) | copy-done | bytes 3670040
  2.7 0.0 copy-start.1
  2.7 0.9 %copy-done.1 = f32[1,8,4096]{2,1,0:T(8,128)S(1)} copy-done((f32[1,8,4096]{2,1,0:T(8,128)S(1)}, f32[1,8,4096]{2,1,0:T(8,128)}, u32[]{:S(2)}) %copy-start.1) | copy-done | bytes 131096
  3.6 0.0 copy-start.2
  3.6 0.9 %copy-done.2 = f32[8,4096]{1,0:T(8,128)S(1)} copy-done((f32[8,4096]{1,0:T(8,128)S(1)}, f32[8,4096]{1,0:T(8,128)}, u32[]{:S(2)}) %copy-start.2) | copy-done | bytes 131096
  4.5 0.0 copy-start.4
  4.5 0.8 %copy-done.4 = bf16[256,128]{1,0:T(8,128)(2,1)S(1)} copy-done((bf16[256,128]{1,0:T(8,128)(2,1)S(1)}, bf16[256,128]{1,0:T(8,128)(2,1)}, u32[]{:S(2)}) %copy-start.4) | copy-done | bytes 65560
  5.3 0.0 copy-start.6
  5.3 0.7 %copy-done.6 = s32[8]{0:T(128)S(1)} copy-done((s32[8]{0:T(128)S(1)}, s32[8]{0:T(128)}, u32[]{:S(2)}) %copy-start.6) | copy-done | bytes 56
  6.0 0.0 copy-start.7
  6.0 0.7 %copy-done.7 = s32[256]{0:T(256)S(1)} copy-done((s32[256]{0:T(256)S(1)}, s32[256]{0:T(256)}, u32[]{:S(2)}) %copy-start.7) | copy-done | bytes 1048
  6.7 0.0 copy-start.3
  6.7 0.0 copy-start.5
  6.7 47.1 %shard_map.128 = (f32[112,128]{1,0:T(8,128)S(1)}, f32[64,128]{1,0:T(8,128)S(1)}, f32[8,128]{1,0:T(8,128)S(1)}) custom-call(bf16[256,7168]{1,0:T(8,128)(2,1)S(1)} %copy-done, bf16[256,128]{1,0:T(8,128)(2,1)S(1)} %copy-done.4, s32[1,256]{1,0:T(1,128)S(1)} %bitcast.1, f32[1,8,4096]{2,1,0:T(8,128)S(1)} %copy-done.1, f32[8,4096]{1,0:T(8,128)S(1)} %copy-done.2, ...), custom_call_target="tpu_custom_call" | custom-call | flops 469762048 | bytes 3670016 | tf_op jit(solution)/shard_map/pallas_call | solution.py:340
  53.7 0.0 copy-done.8
  53.8 0.0 copy-done.3
  53.8 0.0 copy-done.5
  53.8 1.5 %shard_map.129 = (f32[1,112,128]{2,1,0:T(8,128)}, f32[1,112]{1,0:T(1,128)}, f32[1,8,4096]{2,1,0:T(8,128)}, f32[8,4096]{1,0:T(8,128)}, f32[8,4096]{1,0:T(8,128)}) custom-call(s32[8]{0:T(128)S(1)} %copy-done.6, f32[112,128]{1,0:T(8,128)S(1)} %get-tuple-element.8.sum_ref, f32[64,128]{1,0:T(8,128)S(1)} %get-tuple-element.9.avg_ref, ...), custom_call_target="tpu_custom_call" | custom-call | tf_op jit(solution)/shard_map/pallas_call | solution.py:451
Async XLA Ops:
  0.6 53.1 %copy-start.8 = (f32[1,112]{1,0:T(1,128)S(1)}, f32[1,112]{1,0:T(1,128)}, u32[]{:S(2)}) copy-start(f32[1,112]{1,0:T(1,128)} %gain_ref.1) | copy-start | bytes 1348
  0.6 2.0 %copy-start = (bf16[256,7168]{1,0:T(8,128)(2,1)S(1)}, bf16[256,7168]{1,0:T(8,128)(2,1)}, u32[]{:S(2)}) copy-start(bf16[256,7168]{1,0:T(8,128)(2,1)} %tok_hbm.1) | copy-start | bytes 11010052
  2.7 0.9 %copy-start.1 = (f32[1,8,4096]{2,1,0:T(8,128)S(1)}, f32[1,8,4096]{2,1,0:T(8,128)}, u32[]{:S(2)}) copy-start(f32[1,8,4096]{2,1,0:T(8,128)} %loc_ref.1) | copy-start | bytes 393220
  3.6 0.9 %copy-start.2 = (f32[8,4096]{1,0:T(8,128)S(1)}, f32[8,4096]{1,0:T(8,128)}, u32[]{:S(2)}) copy-start(f32[8,4096]{1,0:T(8,128)} %glob_ref.1) | copy-start | bytes 393220
  4.5 0.8 %copy-start.4 = (bf16[256,128]{1,0:T(8,128)(2,1)S(1)}, bf16[256,128]{1,0:T(8,128)(2,1)}, u32[]{:S(2)}) copy-start(bf16[256,128]{1,0:T(8,128)(2,1)} %cot_ref.1) | copy-start | bytes 196612
  5.3 0.7 %copy-start.6 = (s32[8]{0:T(128)S(1)}, s32[8]{0:T(128)}, u32[]{:S(2)}) copy-start(s32[8]{0:T(128)} %order_ref.3) | copy-start | bytes 100
  6.0 0.7 %copy-start.7 = (s32[256]{0:T(256)S(1)}, s32[256]{0:T(256)}, u32[]{:S(2)}) copy-start(s32[256]{0:T(256)} %param.11) | copy-start | bytes 3076
  6.7 47.1 %copy-start.3 = (f32[8,4096]{1,0:T(8,128)S(1)}, f32[8,4096]{1,0:T(8,128)}, u32[]{:S(2)}) copy-start(f32[8,4096]{1,0:T(8,128)} %mom_ref.1) | copy-start | bytes 393220
  6.7 47.1 %copy-start.5 = (bf16[1,112,128]{2,1,0:T(8,128)(2,1)S(1)}, bf16[1,112,128]{2,1,0:T(8,128)(2,1)}, u32[]{:S(2)}) copy-start(bf16[1,112,128]{2,1,0:T(8,128)(2,1)} %weight_ref.1) | copy-start | bytes 86020

commit v2 on v1

v2 whole, which is shorter than its diff:
```python
import functools

import jax
import jax.numpy as jnp
from jax import lax
from jax.experimental import pallas as pl
from jax.experimental.pallas import tpu as pltpu
from jax.sharding import PartitionSpec as P

FRAG = 2

EPSILON = 1e-06
CLIP_RATE = 0.5
MOMENT = 0.9
OUTER_RATE = 0.7
MIX_RATE = 0.5

NY, NX, NZ, NC = 4, 4, 2, 2
LANES = 128
TOKEN_BLOCK = 32
MESH = pl.DeviceIdType.MESH


def far_first(count):
    return sorted(range(count), key=lambda off: (-min(off, count - off), off))


def exchange_kernel(
    replicas,
    tok_hbm,
    cot_hbm,
    mask_hbm,
    loc_hbm,
    glob_hbm,
    order_hbm,
    sum_ref,
    avg_ref,
    sq_ref,
    tok,
    cot,
    mask,
    loc,
    glob,
    order,
    masked,
    part,
    core_out,
    core_in,
    x1_out,
    x1_in,
    y1_out,
    y1_in,
    x2_out,
    x2_in,
    y2_out,
    y2_in,
    z_out,
    z_in,
    delta,
    delta_in,
    sq_out,
    sq_plane,
    sq_line,
    tok_sem,
    arg_sem,
    core_sem,
    x1_sem,
    y1_sem,
    x2_sem,
    y2_sem,
    z_sem,
    rs_sem,
    ag_sem,
    plane_sem,
    line_sem,
):
    rep = lax.axis_index("replica")
    me = lax.axis_index("fsdp")
    core = lax.rem(me, NC)
    z = lax.rem(me // NC, NZ)
    x = lax.rem(me // (NC * NZ), NX)
    y = me // (NC * NZ * NX)

    def device(yy, xx, zz, cc):
        return (rep, ((yy * NX + xx) * NZ + zz) * NC + cc)

    def plane_peer(dy, dx, dc=0):
        return device(lax.rem(y + dy, NY), lax.rem(x + dx, NX), z, lax.rem(core + dc, NC))

    def line_peer(dr, dz):
        return (lax.rem(rep + dr, replicas), device(y, x, lax.rem(z + dz, NZ), core)[1])

    core_peer = plane_peer(0, 0, 1)
    plane = [(dy, dx) for dy in far_first(NY) for dx in far_first(NX) if dy or dx]
    line = [(dr, dz) for dr in range(replicas) for dz in range(NZ) if dr or dz]

    tokens, width = tok.shape
    rows, heads = sum_ref.shape
    chunk = width // NY
    offs = far_first(NY)
    own = offs.index(0)
    x_rows = x1_out.shape[1]
    x_part, y_part = slice(0, x_rows), slice(x_rows, rows)

    arg_copies = [
        pltpu.make_async_copy(src, dst, arg_sem.at[i])
        for i, (src, dst) in enumerate(
            [(cot_hbm, cot), (mask_hbm, mask), (order_hbm, order), (loc_hbm.at[0], loc), (glob_hbm, glob)]
        )
    ]
    token_copies = [
        pltpu.make_async_copy(
            tok_hbm.at[pl.ds(i * TOKEN_BLOCK, TOKEN_BLOCK)],
            tok.at[pl.ds(i * TOKEN_BLOCK, TOKEN_BLOCK)],
            tok_sem.at[i],
        )
        for i in range(tokens // TOKEN_BLOCK)
    ]
    for copy in arg_copies + token_copies:
        copy.start()

    barrier = pltpu.get_barrier_semaphore()
    peers = [line_peer(dr, dz) for dr, dz in line]
    peers += [plane_peer(*offset) for offset in plane] + [core_peer]
    for peer in peers:
        pl.semaphore_signal(barrier, inc=1, device_id=peer, device_id_type=MESH)

    for copy in arg_copies:
        copy.wait()
    per_row = loc.shape[1] // LANES
    for i in range(FRAG):
        layer = order[i]
        diff = glob[pl.ds(layer, 1), :] - loc[pl.ds(layer, 1), :]
        for j in range(per_row):
            delta[i * per_row + j : i * per_row + j + 1, :] = diff[:, j * LANES : (j + 1) * LANES]

    cot_t = cot[...].astype(jnp.float32).T
    keep = jnp.broadcast_to(mask[...] == 1, cot_t.shape)
    masked[...] = jnp.where(keep, cot_t, 0.0).astype(jnp.bfloat16)

    for i, copy in enumerate(token_copies):
        copy.wait()
        for half in range(TOKEN_BLOCK // 16):
            at = pl.ds(i * TOKEN_BLOCK + half * 16, 16)
            sums = [jnp.zeros((16, LANES), jnp.float32) for _ in range(4)]
            for j in range(width // LANES):
                piece = tok[at, j * LANES : (j + 1) * LANES].astype(jnp.float32)
                sums[j % 4] += piece * piece
            total = jnp.sum((sums[0] + sums[1]) + (sums[2] + sums[3]), axis=1, keepdims=True)
            inv_rms = lax.rsqrt(total / width + EPSILON)
            for j in range(width // LANES):
                piece = tok[at, j * LANES : (j + 1) * LANES].astype(jnp.float32)
                tok[at, j * LANES : (j + 1) * LANES] = (piece * inv_rms).astype(jnp.bfloat16)

    pl.semaphore_wait(barrier, len(peers))

    sent = []

    def send(src, dst, sems, index, peer):
        copy = pltpu.make_async_remote_copy(
            src_ref=src,
            dst_ref=dst,
            send_sem=sems.at[0, index],
            recv_sem=sems.at[1, index],
            device_id=peer,
            device_id_type=MESH,
        )
        copy.start()
        sent.append(copy)
        return copy

    shard = delta.shape[0] // replicas
    rs = [
        send(
            delta.at[pl.ds(pl.multiple_of(lax.rem(rep + off, replicas) * shard, 8), shard)],
            delta_in.at[off - 1],
            rs_sem,
            off - 1,
            line_peer(off, 0),
        )
        for off in far_first(replicas)[:-1]
    ]

    def column(k):
        return lax.rem(y + offs[k], NY)

    def side(half):
        return 1 - z if half == 0 else z

    def block_at(yy, xx, zz, cc):
        start = (((yy * NX + xx) * NZ + zz) * NC + cc) * rows
        return pl.multiple_of(start, 16)

    core_copies = {}
    for half in range(2):
        for k in range(NY):
            if half == 0:
                done = 0
                while done < chunk:
                    size = min(256, chunk - done)
                    at = pl.multiple_of(column(k) * chunk + done, LANES)
                    product = jnp.dot(
                        masked[...], tok[:, pl.ds(at, size)], preferred_element_type=jnp.float32
                    )
                    part[pl.ds(at, size), :] = product.T
                    done += size
            slot = half * NY + k
            for xx in range(NX):
                at = block_at(column(k), xx, side(half), 1 - core)
                core_out[slot, xx] = part[pl.ds(at, rows), :].astype(jnp.bfloat16)
            core_copies[slot] = send(core_out.at[slot], core_in.at[slot], core_sem, slot, core_peer)

    def chip_sum(half, k, xx, at):
        start = block_at(column(k), xx, side(half), core) + at.start
        mine = part[pl.ds(start, at.stop - at.start), :]
        return mine + core_in[half * NY + k, xx, at].astype(jnp.float32)

    x1, y1, x2, y2 = {}, {}, {}, {}

    def x1_slot(half, k, off):
        return (half * NY + k) * (NX - 1) + off - 1

    def y_slot(half, off):
        return half * (NY - 1) + off - 1

    def x_slot(half, off):
        return half * (NX - 1) + off - 1

    def spread(half, k):
        core_copies[half * NY + k].wait_recv()
        for off in far_first(NX)[:-1]:
            slot = x1_slot(half, k, off)
            x1_out[slot] = chip_sum(half, k, lax.rem(x + off, NX), x_part).astype(jnp.bfloat16)
            x1[slot] = send(x1_out.at[slot], x1_in.at[slot], x1_sem, slot, plane_peer(0, off))
        if k != own:
            slot = y_slot(half, offs[k])
            for xx in range(NX):
                y1_out[slot, xx] = chip_sum(half, k, xx, y_part).astype(jnp.bfloat16)
            y1[slot] = send(
                y1_out.at[slot], y1_in.at[slot], y1_sem, slot, plane_peer(offs[k], 0)
            )

    def x_sum(half, k):
        total = chip_sum(half, k, x, x_part)
        for off in range(1, NX):
            slot = x1_slot(half, k, off)
            x1[slot].wait_recv()
            total = total + x1_in[slot].astype(jnp.float32)
        return total

    def y_sum(half, xx):
        total = chip_sum(half, own, xx, y_part)
        for off in range(1, NY):
            total = total + y1_in[y_slot(half, off), xx].astype(jnp.float32)
        return total

    def forward(half):
        for k in range(NY):
            if k != own:
                slot = y_slot(half, offs[k])
                x2_out[slot] = x_sum(half, k).astype(jnp.bfloat16)
                x2[slot] = send(
                    x2_out.at[slot], x2_in.at[slot], x2_sem, slot, plane_peer(offs[k], 0)
                )
        for off in range(1, NY):
            y1[y_slot(half, off)].wait_recv()
        for off in far_first(NX)[:-1]:
            slot = x_slot(half, off)
            y2_out[slot] = y_sum(half, lax.rem(x + off, NX)).astype(jnp.bfloat16)
            y2[slot] = send(y2_out.at[slot], y2_in.at[slot], y2_sem, slot, plane_peer(0, off))

    def gather(half):
        top = x_sum(half, own)
        low = y_sum(half, x)
        for off in range(1, NY):
            slot = y_slot(half, off)
            x2[slot].wait_recv()
            top = top + x2_in[slot].astype(jnp.float32)
        for off in range(1, NX):
            slot = x_slot(half, off)
            y2[slot].wait_recv()
            low = low + y2_in[slot].astype(jnp.float32)
        return top, low

    for k in range(NY):
        spread(0, k)

    for copy in rs:
        copy.wait_recv()
    mine = pl.ds(pl.multiple_of(rep * shard, 8), shard)
    total = delta[mine, :]
    for off in range(1, replicas):
        total = total + delta_in[off - 1]
    averaged = total / replicas
    avg_ref[mine, :] = averaged
    sq_out[0] = jnp.sum(averaged * averaged, axis=0, keepdims=True)
    pair_copy = send(sq_out.at[0], sq_plane.at[len(plane)], plane_sem, len(plane), core_peer)
    ag = [
        send(avg_ref.at[mine], avg_ref.at[mine], ag_sem, off - 1, line_peer(off, 0))
        for off in far_first(replicas)[:-1]
    ]
    pair_copy.wait_recv()
    sq_out[1] = sq_out[0] + sq_plane[len(plane)]
    plane_copies = [
        send(sq_out.at[1], sq_plane.at[i], plane_sem, i, plane_peer(*offset))
        for i, offset in enumerate(plane)
    ]
    for k in range(NY):
        spread(1, k)

    forward(0)

    squares = sq_out[1]
    for i, copy in enumerate(plane_copies):
        copy.wait_recv()
        squares = squares + sq_plane[i]
    sq_out[2] = squares
    place = rep * NZ + z
    sq_line[place] = squares
    line_copies = [
        send(sq_out.at[2], sq_line.at[place], line_sem, i, line_peer(dr, dz))
        for i, (dr, dz) in enumerate(line)
    ]

    top, low = gather(0)
    z_out[x_part] = top.astype(jnp.bfloat16)
    z_out[y_part] = low.astype(jnp.bfloat16)
    z_copy = send(z_out, z_in, z_sem, 0, line_peer(0, 1))

    forward(1)
    top, low = gather(1)
    for copy in ag:
        copy.wait_recv()
    for copy in line_copies:
        copy.wait_recv()
    squares = sq_line[0]
    for i in range(1, replicas * NZ):
        squares = squares + sq_line[i]
    sq_ref[...] = squares

    z_copy.wait_recv()
    sum_ref[x_part] = top + z_in[x_part].astype(jnp.float32)
    sum_ref[y_part] = low + z_in[y_part].astype(jnp.float32)
    for copy in sent:
        copy.wait_send()


def exchange(tokens, cotangent, keep_mask, local_params, global_params, order, rows, replicas):
    count, width = tokens.shape
    heads = cotangent.shape[1]
    held, params = global_params.shape
    lines = FRAG * params // LANES
    vmem = pl.BlockSpec(memory_space=pltpu.VMEM)
    hbm = pl.BlockSpec(memory_space=pltpu.HBM)
    bf16, f32 = jnp.bfloat16, jnp.float32
    x_rows = (rows // 16 + 1) // 2 * 16
    x_block, y_block = (x_rows, heads), (rows - x_rows, heads)
    peers = NY * NX - 1
    members = replicas * NZ
    return pl.pallas_call(
        functools.partial(exchange_kernel, replicas),
        out_shape=(
            jax.ShapeDtypeStruct((rows, heads), f32),
            jax.ShapeDtypeStruct((lines, LANES), f32),
            jax.ShapeDtypeStruct((1, LANES), f32),
        ),
        in_specs=[hbm] * 6,
        out_specs=(vmem, vmem, vmem),
        scratch_shapes=[
            pltpu.VMEM((count, width), bf16),
            pltpu.VMEM((count, heads), bf16),
            pltpu.VMEM((1, count), jnp.int32),
            pltpu.VMEM((held, params), f32),
            pltpu.VMEM((held, params), f32),
            pltpu.SMEM(order.shape, jnp.int32),
            pltpu.VMEM((heads, count), bf16),
            pltpu.VMEM((width, heads), f32),
            pltpu.VMEM((2 * NY, NX, rows, heads), bf16),
            pltpu.VMEM((2 * NY, NX, rows, heads), bf16),
            pltpu.VMEM((2 * NY * (NX - 1),) + x_block, bf16),
            pltpu.VMEM((2 * NY * (NX - 1),) + x_block, bf16),
            pltpu.VMEM((2 * (NY - 1), NX) + y_block, bf16),
            pltpu.VMEM((2 * (NY - 1), NX) + y_block, bf16),
            pltpu.VMEM((2 * (NY - 1),) + x_block, bf16),
            pltpu.VMEM((2 * (NY - 1),) + x_block, bf16),
            pltpu.VMEM((2 * (NX - 1),) + y_block, bf16),
            pltpu.VMEM((2 * (NX - 1),) + y_block, bf16),
            pltpu.VMEM((rows, heads), bf16),
            pltpu.VMEM((rows, heads), bf16),
            pltpu.VMEM((lines, LANES), f32),
            pltpu.VMEM((replicas - 1, lines // replicas, LANES), f32),
            pltpu.VMEM((3, 1, LANES), f32),
            pltpu.VMEM((peers + 1, 1, LANES), f32),
            pltpu.VMEM((members, 1, LANES), f32),
            pltpu.SemaphoreType.DMA((count // TOKEN_BLOCK,)),
            pltpu.SemaphoreType.DMA((5,)),
            pltpu.SemaphoreType.DMA((2, 2 * NY)),
            pltpu.SemaphoreType.DMA((2, 2 * NY * (NX - 1))),
            pltpu.SemaphoreType.DMA((2, 2 * (NY - 1))),
            pltpu.SemaphoreType.DMA((2, 2 * (NY - 1))),
            pltpu.SemaphoreType.DMA((2, 2 * (NX - 1))),
            pltpu.SemaphoreType.DMA((2, 1)),
            pltpu.SemaphoreType.DMA((2, replicas - 1)),
            pltpu.SemaphoreType.DMA((2, replicas - 1)),
            pltpu.SemaphoreType.DMA((2, peers + 1)),
            pltpu.SemaphoreType.DMA((2, members - 1)),
        ],
        compiler_params=pltpu.CompilerParams(
            collective_id=0, has_side_effects=True, vmem_limit_bytes=63 * 1024 * 1024
        ),
        cost_estimate=pl.CostEstimate(
            flops=2 * count * width * heads, bytes_accessed=2 * count * width, transcendentals=0
        ),
    )(tokens, cotangent, keep_mask.reshape(1, count), local_params, global_params, order)


def finish_kernel(
    count,
    order_hbm,
    sum_hbm,
    avg_hbm,
    sq_hbm,
    weight_hbm,
    gain_hbm,
    loc_hbm,
    glob_hbm,
    mom_hbm,
    weight_out,
    gain_out,
    loc_out,
    glob_out,
    mom_out,
    order,
    total,
    avg,
    sq,
    weight,
    gain,
    loc,
    glob,
    mom,
    weight_new,
    gain_new,
    loc_new,
    glob_new,
    mom_new,
    in_sem,
    out_sem,
):
    pairs = [
        (avg_hbm, avg),
        (sq_hbm, sq),
        (loc_hbm.at[0], loc),
        (glob_hbm, glob),
        (mom_hbm, mom),
        (order_hbm, order),
        (sum_hbm, total),
        (weight_hbm.at[0], weight),
        (gain_hbm, gain),
    ]
    loads = [pltpu.make_async_copy(src, dst, in_sem.at[i]) for i, (src, dst) in enumerate(pairs)]
    for copy in loads:
        copy.start()
    for copy in loads:
        copy.wait()

    squares = jnp.sum(sq[...])
    limit = CLIP_RATE * jnp.sqrt(jnp.float32(count))
    factor = jnp.minimum(1.0, limit / jnp.sqrt(jnp.full((8, LANES), squares) + EPSILON))
    held, params = glob.shape
    layer = lax.broadcasted_iota(jnp.int32, (held, LANES), 0)
    first = layer == order[0]
    second = layer == order[1]
    picked = first | second
    lines = params // LANES
    stores = []

    def store(src, dst, index):
        copy = pltpu.make_async_copy(src, dst, out_sem.at[index])
        copy.start()
        stores.append(copy)

    parts = 2
    for part in range(parts):
        for j in range(part * lines // parts, (part + 1) * lines // parts):
            at = slice(j * LANES, (j + 1) * LANES)
            averaged = jnp.where(
                first,
                jnp.broadcast_to(avg[j : j + 1, :], (held, LANES)),
                jnp.broadcast_to(avg[lines + j : lines + j + 1, :], (held, LANES)),
            )
            old_loc, old_glob, old_mom = loc[:, at], glob[:, at], mom[:, at]
            clipped = averaged * factor
            moment_new = MOMENT * old_mom + clipped
            global_new = old_glob - OUTER_RATE * (clipped + MOMENT * moment_new)
            merged = MIX_RATE * old_loc + (1.0 - MIX_RATE) * global_new
            loc_new[:, at] = jnp.where(picked, merged, old_loc)
            glob_new[:, at] = jnp.where(picked, global_new, old_glob)
            mom_new[:, at] = jnp.where(picked, moment_new, old_mom)
        span = pl.ds(part * params // parts, params // parts)
        store(loc_new.at[:, span], loc_out.at[0, :, span], 3 * part)
        store(glob_new.at[:, span], glob_out.at[:, span], 3 * part + 1)
        store(mom_new.at[:, span], mom_out.at[:, span], 3 * part + 2)

    summed = total[...]
    rows, heads = summed.shape
    scale = jnp.broadcast_to(gain[...], (heads, rows)).T
    weight_new[...] = scale * summed
    store(weight_new, weight_out.at[0], 3 * parts)
    product = weight[...].astype(jnp.float32) * summed
    gain_new[...] = jnp.sum(product.T, axis=0, keepdims=True)
    store(gain_new, gain_out, 3 * parts + 1)
    for copy in stores:
        copy.wait()


def finish(order, total, averaged, squares, weight, gain, local_params, global_params, momentum, count):
    hbm = pl.BlockSpec(memory_space=pltpu.HBM)
    f32 = jnp.float32
    shapes = (
        jax.ShapeDtypeStruct(weight.shape, f32),
        jax.ShapeDtypeStruct(gain.shape, f32),
        jax.ShapeDtypeStruct(local_params.shape, f32),
        jax.ShapeDtypeStruct(global_params.shape, f32),
        jax.ShapeDtypeStruct(momentum.shape, f32),
    )
    state = pltpu.VMEM(global_params.shape, f32)
    return pl.pallas_call(
        functools.partial(finish_kernel, count),
        out_shape=shapes,
        in_specs=[hbm] * 9,
        out_specs=(hbm,) * 5,
        scratch_shapes=[
            pltpu.SMEM(order.shape, jnp.int32),
            pltpu.VMEM(total.shape, f32),
            pltpu.VMEM(averaged.shape, f32),
            pltpu.VMEM(squares.shape, f32),
            pltpu.VMEM(weight.shape[1:], weight.dtype),
            pltpu.VMEM(gain.shape, f32),
            state,
            state,
            state,
            pltpu.VMEM(weight.shape[1:], f32),
            pltpu.VMEM(gain.shape, f32),
            state,
            state,
            state,
            pltpu.SemaphoreType.DMA((9,)),
            pltpu.SemaphoreType.DMA((8,)),
        ],
        compiler_params=pltpu.CompilerParams(vmem_limit_bytes=63 * 1024 * 1024),
    )(order, total, averaged, squares, weight, gain, local_params, global_params, momentum)


def per_device(
    replicas,
    fsdp,
    tokens,
    cotangent,
    keep_mask,
    key_weight,
    norm_gain,
    local_params,
    global_params,
    momentum,
    fragment_order,
):
    total, averaged, squares = exchange(
        tokens,
        cotangent,
        keep_mask,
        local_params,
        global_params,
        fragment_order,
        key_weight.shape[1],
        replicas,
    )
    count = FRAG * global_params.shape[1] * fsdp
    return finish(
        fragment_order,
        total,
        averaged,
        squares,
        key_weight,
        norm_gain,
        local_params,
        global_params,
        momentum,
        count,
    )


def solution(mesh):
    in_specs = (
        P(("replica", "fsdp"), None),
        P(("replica", "fsdp"), None),
        P(("replica", "fsdp")),
        P("replica", "fsdp", None),
        P("replica", "fsdp"),
        P("replica", None, "fsdp"),
        P(None, "fsdp"),
        P(None, "fsdp"),
        P(),
    )
    out_specs = (
        P("replica", "fsdp", None),
        P("replica", "fsdp"),
        P("replica", None, "fsdp"),
        P(None, "fsdp"),
        P(None, "fsdp"),
    )
    return jax.shard_map(
        functools.partial(per_device, mesh.shape["replica"], mesh.shape["fsdp"]),
        mesh=mesh,
        in_specs=in_specs,
        out_specs=out_specs,
        check_vma=False,
    )
```

time: 55.5 us -> 40.7 us (0.73)
  Pallas kernels: 48.5 us -> 39.9 us
  local copies, waits for them, and re-layouts: 6.03 us -> 0 us
    pallas_call x1, Pallas kernels: 47.1 us -> 37.8 us  [exchange(): pl.pallas_call(functools.partial(exchange_kernel, replicas), out_shape=(j...]
    unnamed x18 -> x0, local copies, waits for them, and re-layouts: 6.03 us -> none
    pallas_call x1, Pallas kernels: 1.49 us -> 2.13 us  [finish(): pl.pallas_call(functools.partial(finish_kernel, count), out_shape=shapes,...]
where the time goes in v2:
time: 40.7 us; the launch traced here: 40.5 us
  Pallas kernels  39.9 us (98%)
  between operations  0.64 us (2%)
    pallas_call x1, Pallas kernels, exchange(): pl.pallas_call(functools.partial(exchange_kernel, replicas), out_shape=(j...  37.8 us
    pallas_call x1, Pallas kernels, finish(): pl.pallas_call(functools.partial(finish_kernel, count), out_shape=shapes,...  2.13 us

profile of v2, /device:TPU:1, one launch (start us, length us, event | category | flops | bytes accessed | tf_op | source)
XLA Modules:
  0.0 40.5 jit_solution(15050082735368733067)
XLA Ops:
  0.6 37.8 %shard_map.128 = (f32[112,128]{1,0:T(8,128)}, f32[64,128]{1,0:T(8,128)}, f32[1,128]{1,0:T(1,128)}) custom-call(bf16[256,7168]{1,0:T(8,128)(2,1)} %tok_hbm.1, bf16[256,128]{1,0:T(8,128)(2,1)} %cot_hbm.1, s32[1,256]{1,0:T(1,128)} %bitcast.1, f32[1,8,4096]{2,1,0:T(8,128)} %loc_hbm.3, f32[8,4096]{1,0:T(8,128)} %glob_hbm.3, s32[8]{0:T(128)} %order_hbm.3), custom_call_target="tpu_custom_call" | custom-call | flops 469762048 | bytes 3670016 | tf_op jit(solution)/shard_map/pallas_call | solution.py:360
  38.4 2.1 %shard_map.129 = (f32[1,112,128]{2,1,0:T(8,128)}, f32[1,112]{1,0:T(1,128)}, f32[1,8,4096]{2,1,0:T(8,128)}, f32[8,4096]{1,0:T(8,128)}, f32[8,4096]{1,0:T(8,128)}) custom-call(s32[8]{0:T(128)} %order_hbm.3, f32[112,128]{1,0:T(8,128)} %get-tuple-element.8.sum_hbm, f32[64,128]{1,0:T(8,128)} %get-tuple-element.9.avg_hbm, f32[1,128]{1,0:T(1,128)} %get-tuple-element.10.sq_hbm, ...), custom_call_target="tpu_custom_call" | custom-call | tf_op jit(solution)/shard_map/pallas_call | solution.py:528

commit v3 on v2

--- a/solution.py
+++ b/solution.py
@@ -18,6 +18,7 @@
 NY, NX, NZ, NC = 4, 4, 2, 2
 LANES = 128
 TOKEN_BLOCK = 32
+OWNERS = 4
 MESH = pl.DeviceIdType.MESH
 
 
@@ -87,12 +88,19 @@
     def plane_peer(dy, dx, dc=0):
         return device(lax.rem(y + dy, NY), lax.rem(x + dx, NX), z, lax.rem(core + dc, NC))
 
-    def line_peer(dr, dz):
-        return (lax.rem(rep + dr, replicas), device(y, x, lax.rem(z + dz, NZ), core)[1])
-
     core_peer = plane_peer(0, 0, 1)
     plane = [(dy, dx) for dy in far_first(NY) for dx in far_first(NX) if dy or dx]
-    line = [(dr, dz) for dr in range(replicas) for dz in range(NZ) if dr or dz]
+
+    owners = min(OWNERS, replicas)
+    first = (replicas - owners) // 2
+    place = rep - first
+    owns = (place >= 0) & (place < owners)
+
+    def line_device(r, zz):
+        return (r, device(y, x, zz, core)[1])
+
+    def other(r, zz):
+        return (rep != r) | (z != zz)
 
     tokens, width = tok.shape
     rows, heads = sum_ref.shape
@@ -120,10 +128,23 @@
         copy.start()
 
     barrier = pltpu.get_barrier_semaphore()
-    peers = [line_peer(dr, dz) for dr, dz in line]
-    peers += [plane_peer(*offset) for offset in plane] + [core_peer]
+    z_peer = line_device(rep, 1 - z)
+    peers = [z_peer] + [plane_peer(*offset) for offset in plane] + [core_peer]
     for peer in peers:
         pl.semaphore_signal(barrier, inc=1, device_id=peer, device_id_type=MESH)
+    for r in range(replicas):
+        for zz in range(NZ):
+            meets = rep != r
+            if not first <= r < first + owners:
+                meets = meets & owns
+
+            @pl.when(meets)
+            def _():
+                pl.semaphore_signal(
+                    barrier, inc=1, device_id=line_device(r, zz), device_id_type=MESH
+                )
+
+    line_count = NZ * jnp.where(owns, replicas - 1, owners)
 
     for copy in arg_copies:
         copy.wait()
@@ -152,66 +173,110 @@
                 piece = tok[at, j * LANES : (j + 1) * LANES].astype(jnp.float32)
                 tok[at, j * LANES : (j + 1) * LANES] = (piece * inv_rms).astype(jnp.bfloat16)
 
-    pl.semaphore_wait(barrier, len(peers))
+    def column(k):
+        return lax.rem(y + offs[k], NY)
+
+    def block_at(yy, xx, zz, cc):
+        start = (((yy * NX + xx) * NZ + zz) * NC + cc) * rows
+        return pl.multiple_of(start, 16)
+
+    for k in range(NY):
+        done = 0
+        while done < chunk:
+            size = min(256, chunk - done)
+            at = pl.multiple_of(column(k) * chunk + done, LANES)
+            product = jnp.dot(
+                masked[...], tok[:, pl.ds(at, size)], preferred_element_type=jnp.float32
+            )
+            part[pl.ds(at, size), :] = product.T
+            done += size
+        for xx in range(NX):
+            at = block_at(column(k), xx, 0, 1 - core)
+            core_out[k, xx] = part[pl.ds(at, rows), :].astype(jnp.bfloat16)
+
+    pl.semaphore_wait(barrier, len(peers) + line_count)
 
     sent = []
 
-    def send(src, dst, sems, index, peer):
-        copy = pltpu.make_async_remote_copy(
+    def remote(src, dst, sems, out, into, peer):
+        return pltpu.make_async_remote_copy(
             src_ref=src,
             dst_ref=dst,
-            send_sem=sems.at[0, index],
-            recv_sem=sems.at[1, index],
+            send_sem=sems.at[0, out],
+            recv_sem=sems.at[1, into],
             device_id=peer,
             device_id_type=MESH,
         )
+
+    def send(src, dst, sems, index, peer):
+        copy = remote(src, dst, sems, index, index, peer)
         copy.start()
         sent.append(copy)
         return copy
 
-    shard = delta.shape[0] // replicas
+    core_copies = {}
+    for slot in range(NY):
+        core_copies[slot] = send(core_out.at[slot], core_in.at[slot], core_sem, slot, core_peer)
+
+    shard = delta.shape[0] // owners
     rs = [
-        send(
-            delta.at[pl.ds(pl.multiple_of(lax.rem(rep + off, replicas) * shard, 8), shard)],
-            delta_in.at[off - 1],
+        remote(
+            delta.at[pl.ds(q * shard, shard)],
+            delta_in.at[rep],
             rs_sem,
-            off - 1,
-            line_peer(off, 0),
+            q,
+            rep,
+            line_device(first + q, z),
         )
-        for off in far_first(replicas)[:-1]
-    ]
-
-    def column(k):
-        return lax.rem(y + offs[k], NY)
-
-    def side(half):
-        return 1 - z if half == 0 else z
-
-    def block_at(yy, xx, zz, cc):
-        start = (((yy * NX + xx) * NZ + zz) * NC + cc) * rows
-        return pl.multiple_of(start, 16)
-
-    core_copies = {}
-    for half in range(2):
-        for k in range(NY):
-            if half == 0:
-                done = 0
-                while done < chunk:
-                    size = min(256, chunk - done)
-                    at = pl.multiple_of(column(k) * chunk + done, LANES)
-                    product = jnp.dot(
-                        masked[...], tok[:, pl.ds(at, size)], preferred_element_type=jnp.float32
-                    )
-                    part[pl.ds(at, size), :] = product.T
-                    done += size
-            slot = half * NY + k
-            for xx in range(NX):
-                at = block_at(column(k), xx, side(half), 1 - core)
-                core_out[slot, xx] = part[pl.ds(at, rows), :].astype(jnp.bfloat16)
-            core_copies[slot] = send(core_out.at[slot], core_in.at[slot], core_sem, slot, core_peer)
+        for q in range(owners)
+    ]
+    rs_in = [
+        remote(delta.at[pl.ds(0, shard)], delta_in.at[r], rs_sem, 0, r, z_peer)
+        for r in range(replicas)
+    ]
+
+    def shard_at(q):
+        return avg_ref.at[pl.ds(pl.multiple_of(q * shard, 8), shard)]
+
+    ag = [
+        remote(shard_at(place), shard_at(place), ag_sem, r, place, line_device(r, z))
+        for r in range(replicas)
+    ]
+    ag_in = [
+        remote(shard_at(q), shard_at(q), ag_sem, 0, q, z_peer) for q in range(owners)
+    ]
+    pair_copy = remote(
+        sq_out.at[0], sq_plane.at[len(plane)], plane_sem, len(plane), len(plane), core_peer
+    )
+    plane_copies = [
+        remote(sq_out.at[1], sq_plane.at[i], plane_sem, i, i, plane_peer(*offset))
+        for i, offset in enumerate(plane)
+    ]
+    seat = place * NZ + z
+    line = [
+        remote(sq_out.at[2], sq_line.at[seat], line_sem, r * NZ + zz, seat, line_device(r, zz))
+        for r in range(replicas)
+        for zz in range(NZ)
+    ]
+    line_in = [
+        remote(sq_out.at[2], sq_line.at[i], line_sem, 0, i, z_peer) for i in range(owners * NZ)
+    ]
+
+    for q in range(owners):
+
+        @pl.when(rep != first + q)
+        def _():
+            rs[q].start()
+
+    for k in range(NY):
+        slot = NY + k
+        for xx in range(NX):
+            at = block_at(column(k), xx, 1, 1 - core)
+            core_out[slot, xx] = part[pl.ds(at, rows), :].astype(jnp.bfloat16)
+        core_copies[slot] = send(core_out.at[slot], core_in.at[slot], core_sem, slot, core_peer)
 
     def chip_sum(half, k, xx, at):
-        start = block_at(column(k), xx, side(half), core) + at.start
+        start = block_at(column(k), xx, half, core) + at.start
         mine = part[pl.ds(start, at.stop - at.start), :]
         return mine + core_in[half * NY + k, xx, at].astype(jnp.float32)
 
@@ -285,64 +350,115 @@
     for k in range(NY):
         spread(0, k)
 
-    for copy in rs:
-        copy.wait_recv()
-    mine = pl.ds(pl.multiple_of(rep * shard, 8), shard)
-    total = delta[mine, :]
-    for off in range(1, replicas):
-        total = total + delta_in[off - 1]
-    averaged = total / replicas
-    avg_ref[mine, :] = averaged
-    sq_out[0] = jnp.sum(averaged * averaged, axis=0, keepdims=True)
-    pair_copy = send(sq_out.at[0], sq_plane.at[len(plane)], plane_sem, len(plane), core_peer)
-    ag = [
-        send(avg_ref.at[mine], avg_ref.at[mine], ag_sem, off - 1, line_peer(off, 0))
-        for off in far_first(replicas)[:-1]
-    ]
-    pair_copy.wait_recv()
-    sq_out[1] = sq_out[0] + sq_plane[len(plane)]
-    plane_copies = [
-        send(sq_out.at[1], sq_plane.at[i], plane_sem, i, plane_peer(*offset))
-        for i, offset in enumerate(plane)
-    ]
+    @pl.when(owns)
+    def _():
+        delta_in[rep] = delta[pl.ds(pl.multiple_of(place * shard, 8), shard), :]
+        for r in range(replicas):
+
+            @pl.when(rep != r)
+            def _():
+                rs_in[r].wait_recv()
+
+        total = delta_in[0]
+        for r in range(1, replicas):
+            total = total + delta_in[r]
+        averaged = total / replicas
+        avg_ref[pl.ds(pl.multiple_of(place * shard, 8), shard), :] = averaged
+        sq_out[0] = jnp.sum(averaged * averaged, axis=0, keepdims=True)
+        pair_copy.start()
+        for r in range(replicas):
+
+            @pl.when(rep != r)
+            def _():
+                ag[r].start()
+
+        pair_copy.wait_recv()
+        sq_out[1] = sq_out[0] + sq_plane[len(plane)]
+        for copy in plane_copies:
+            copy.start()
+
+    forward(0)
     for k in range(NY):
         spread(1, k)
 
-    forward(0)
-
-    squares = sq_out[1]
-    for i, copy in enumerate(plane_copies):
-        copy.wait_recv()
-        squares = squares + sq_plane[i]
-    sq_out[2] = squares
-    place = rep * NZ + z
-    sq_line[place] = squares
-    line_copies = [
-        send(sq_out.at[2], sq_line.at[place], line_sem, i, line_peer(dr, dz))
-        for i, (dr, dz) in enumerate(line)
-    ]
-
-    top, low = gather(0)
-    z_out[x_part] = top.astype(jnp.bfloat16)
-    z_out[y_part] = low.astype(jnp.bfloat16)
-    z_copy = send(z_out, z_in, z_sem, 0, line_peer(0, 1))
-
+    @pl.when(owns)
+    def _():
+        squares = sq_out[1]
+        for i, copy in enumerate(plane_copies):
+            copy.wait_recv()
+            squares = squares + sq_plane[i]
+        sq_out[2] = squares
+        sq_line[seat] = squares
+        for r in range(replicas):
+            for zz in range(NZ):
+
+                @pl.when(other(r, zz))
+                def _():
+                    line[r * NZ + zz].start()
+
+    z_copy = remote(z_out, z_in, z_sem, 0, 0, z_peer)
+
+    def settle(half):
+        top, low = gather(half)
+
+        @pl.when(z == half)
+        def _():
+            sum_ref[x_part] = top
+            sum_ref[y_part] = low
+
+        @pl.when(z != half)
+        def _():
+            z_out[x_part] = top.astype(jnp.bfloat16)
+            z_out[y_part] = low.astype(jnp.bfloat16)
+            z_copy.start()
+
+    settle(0)
     forward(1)
-    top, low = gather(1)
-    for copy in ag:
-        copy.wait_recv()
-    for copy in line_copies:
-        copy.wait_recv()
+    settle(1)
+    for q in range(owners):
+
+        @pl.when(rep != first + q)
+        def _():
+            ag_in[q].wait_recv()
+
+        for zz in range(NZ):
+
+            @pl.when(other(first + q, zz))
+            def _():
+                line_in[q * NZ + zz].wait_recv()
+
     squares = sq_line[0]
-    for i in range(1, replicas * NZ):
+    for i in range(1, owners * NZ):
         squares = squares + sq_line[i]
     sq_ref[...] = squares
 
     z_copy.wait_recv()
-    sum_ref[x_part] = top + z_in[x_part].astype(jnp.float32)
-    sum_ref[y_part] = low + z_in[y_part].astype(jnp.float32)
+    sum_ref[...] = sum_ref[...] + z_in[...].astype(jnp.float32)
+    z_copy.wait_send()
     for copy in sent:
         copy.wait_send()
+    for q in range(owners):
+
+        @pl.when(rep != first + q)
+        def _():
+            rs[q].wait_send()
+
+    @pl.when(owns)
+    def _():
+        pair_copy.wait_send()
+        for copy in plane_copies:
+            copy.wait_send()
+        for r in range(replicas):
+
+            @pl.when(rep != r)
+            def _():
+                ag[r].wait_send()
+
+            for zz in range(NZ):
+
+                @pl.when(other(r, zz))
+                def _():
+                    line[r * NZ + zz].wait_send()
 
 
 def exchange(tokens, cotangent, keep_mask, local_params, global_params, order, rows, replicas):
@@ -356,7 +472,7 @@
     x_rows = (rows // 16 + 1) // 2 * 16
     x_block, y_block = (x_rows, heads), (rows - x_rows, heads)
     peers = NY * NX - 1
-    members = replicas * NZ
+    owners = min(OWNERS, replicas)
     return pl.pallas_call(
         functools.partial(exchange_kernel, replicas),
         out_shape=(
@@ -388,10 +504,10 @@
             pltpu.VMEM((rows, heads), bf16),
             pltpu.VMEM((rows, heads), bf16),
             pltpu.VMEM((lines, LANES), f32),
-            pltpu.VMEM((replicas - 1, lines // replicas, LANES), f32),
+            pltpu.VMEM((replicas, lines // owners, LANES), f32),
             pltpu.VMEM((3, 1, LANES), f32),
             pltpu.VMEM((peers + 1, 1, LANES), f32),
-            pltpu.VMEM((members, 1, LANES), f32),
+            pltpu.VMEM((owners * NZ, 1, LANES), f32),
             pltpu.SemaphoreType.DMA((count // TOKEN_BLOCK,)),
             pltpu.SemaphoreType.DMA((5,)),
             pltpu.SemaphoreType.DMA((2, 2 * NY)),
@@ -400,10 +516,10 @@
             pltpu.SemaphoreType.DMA((2, 2 * (NY - 1))),
             pltpu.SemaphoreType.DMA((2, 2 * (NX - 1))),
             pltpu.SemaphoreType.DMA((2, 1)),
-            pltpu.SemaphoreType.DMA((2, replicas - 1)),
-            pltpu.SemaphoreType.DMA((2, replicas - 1)),
+            pltpu.SemaphoreType.DMA((2, replicas)),
+            pltpu.SemaphoreType.DMA((2, replicas)),
             pltpu.SemaphoreType.DMA((2, peers + 1)),
-            pltpu.SemaphoreType.DMA((2, members - 1)),
+            pltpu.SemaphoreType.DMA((2, replicas * NZ)),
         ],
         compiler_params=pltpu.CompilerParams(
             collective_id=0, has_side_effects=True, vmem_limit_bytes=63 * 1024 * 1024

time: 40.7 us -> 38.6 us (0.948)
  Pallas kernels: 39.9 us -> 37.8 us
    pallas_call x1, Pallas kernels: 37.8 us -> 35.7 us  [exchange(): pl.pallas_call(functools.partial(exchange_kernel, replicas), out_shape=(j...]
where the time goes in v3:
time: 38.6 us; the launch traced here: 38.5 us
  Pallas kernels  37.8 us (98%)
  between operations  0.64 us (2%)
    pallas_call x1, Pallas kernels, exchange(): pl.pallas_call(functools.partial(exchange_kernel, replicas), out_shape=(j...  35.7 us
    pallas_call x1, Pallas kernels, finish(): pl.pallas_call(functools.partial(finish_kernel, count), out_shape=shapes,...  2.13 us

profile of v3, /device:TPU:1, one launch (start us, length us, event | category | flops | bytes accessed | tf_op | source)
XLA Modules:
  0.0 38.5 jit_solution(4236905105299255861)
XLA Ops:
  0.6 35.7 %shard_map.128 = (f32[112,128]{1,0:T(8,128)}, f32[64,128]{1,0:T(8,128)}, f32[1,128]{1,0:T(1,128)}) custom-call(bf16[256,7168]{1,0:T(8,128)(2,1)} %tok_hbm.1, bf16[256,128]{1,0:T(8,128)(2,1)} %cot_hbm.1, s32[1,256]{1,0:T(1,128)} %bitcast.1, f32[1,8,4096]{2,1,0:T(8,128)} %loc_hbm.3, f32[8,4096]{1,0:T(8,128)} %glob_hbm.3, s32[8]{0:T(128)} %order_hbm.3), custom_call_target="tpu_custom_call" | custom-call | flops 469762048 | bytes 3670016 | tf_op jit(solution)/shard_map/pallas_call | solution.py:476
  36.4 2.1 %shard_map.129 = (f32[1,112,128]{2,1,0:T(8,128)}, f32[1,112]{1,0:T(1,128)}, f32[1,8,4096]{2,1,0:T(8,128)}, f32[8,4096]{1,0:T(8,128)}, f32[8,4096]{1,0:T(8,128)}) custom-call(s32[8]{0:T(128)} %order_hbm.3, f32[112,128]{1,0:T(8,128)} %get-tuple-element.8.sum_hbm, f32[64,128]{1,0:T(8,128)} %get-tuple-element.9.avg_hbm, f32[1,128]{1,0:T(1,128)} %get-tuple-element.10.sq_hbm, ...), custom_call_target="tpu_custom_call" | custom-call | tf_op jit(solution)/shard_map/pallas_call | solution.py:644

commit v4 on v3

--- a/solution.py
+++ b/solution.py
@@ -18,6 +18,7 @@
 NY, NX, NZ, NC = 4, 4, 2, 2
 LANES = 128
 TOKEN_BLOCK = 32
+TOKEN_WINDOW = 5
 OWNERS = 4
 MESH = pl.DeviceIdType.MESH
 
@@ -124,7 +125,7 @@
         )
         for i in range(tokens // TOKEN_BLOCK)
     ]
-    for copy in arg_copies + token_copies:
+    for copy in arg_copies + token_copies[:TOKEN_WINDOW]:
         copy.start()
 
     barrier = pltpu.get_barrier_semaphore()
@@ -161,6 +162,8 @@
 
     for i, copy in enumerate(token_copies):
         copy.wait()
+        if i + TOKEN_WINDOW < len(token_copies):
+            token_copies[i + TOKEN_WINDOW].start()
         for half in range(TOKEN_BLOCK // 16):
             at = pl.ds(i * TOKEN_BLOCK + half * 16, 16)
             sums = [jnp.zeros((16, LANES), jnp.float32) for _ in range(4)]
@@ -432,9 +435,6 @@
         squares = squares + sq_line[i]
     sq_ref[...] = squares
 
-    z_copy.wait_recv()
-    sum_ref[...] = sum_ref[...] + z_in[...].astype(jnp.float32)
-    z_copy.wait_send()
     for copy in sent:
         copy.wait_send()
     for q in range(owners):
@@ -459,6 +459,10 @@
                 @pl.when(other(r, zz))
                 def _():
                     line[r * NZ + zz].wait_send()
+
+    z_copy.wait_recv()
+    sum_ref[...] = sum_ref[...] + z_in[...].astype(jnp.float32)
+    z_copy.wait_send()
 
 
 def exchange(tokens, cotangent, keep_mask, local_params, global_params, order, rows, replicas):

time: 38.6 us -> 38.4 us (level)
  no operation moved by 1% of the time
where the time goes in v4:
time: 38.4 us; the launch traced here: 38.2 us
  Pallas kernels  37.6 us (98%)
  between operations  0.64 us (2%)
    pallas_call x1, Pallas kernels, exchange(): pl.pallas_call(functools.partial(exchange_kernel, replicas), out_shape=(j...  35.5 us
    pallas_call x1, Pallas kernels, finish(): pl.pallas_call(functools.partial(finish_kernel, count), out_shape=shapes,...  2.13 us

profile of v4, /device:TPU:1, one launch (start us, length us, event | category | flops | bytes accessed | tf_op | source)
XLA Modules:
  0.0 38.2 jit_solution(10086195755391804652)
XLA Ops:
  0.6 35.5 %shard_map.128 = (f32[112,128]{1,0:T(8,128)}, f32[64,128]{1,0:T(8,128)}, f32[1,128]{1,0:T(1,128)}) custom-call(bf16[256,7168]{1,0:T(8,128)(2,1)} %tok_hbm.1, bf16[256,128]{1,0:T(8,128)(2,1)} %cot_hbm.1, s32[1,256]{1,0:T(1,128)} %bitcast.1, f32[1,8,4096]{2,1,0:T(8,128)} %loc_hbm.3, f32[8,4096]{1,0:T(8,128)} %glob_hbm.3, s32[8]{0:T(128)} %order_hbm.3), custom_call_target="tpu_custom_call" | custom-call | flops 469762048 | bytes 3670016 | tf_op jit(solution)/shard_map/pallas_call | solution.py:480
  36.1 2.1 %shard_map.129 = (f32[1,112,128]{2,1,0:T(8,128)}, f32[1,112]{1,0:T(1,128)}, f32[1,8,4096]{2,1,0:T(8,128)}, f32[8,4096]{1,0:T(8,128)}, f32[8,4096]{1,0:T(8,128)}) custom-call(s32[8]{0:T(128)} %order_hbm.3, f32[112,128]{1,0:T(8,128)} %get-tuple-element.8.sum_hbm, f32[64,128]{1,0:T(8,128)} %get-tuple-element.9.avg_hbm, f32[1,128]{1,0:T(1,128)} %get-tuple-element.10.sq_hbm, ...), custom_call_target="tpu_custom_call" | custom-call | tf_op jit(solution)/shard_map/pallas_call | solution.py:648

commit v5 on v4

--- a/solution.py
+++ b/solution.py
@@ -94,8 +94,8 @@
 
     owners = min(OWNERS, replicas)
     first = (replicas - owners) // 2
-    place = rep - first
-    owns = (place >= 0) & (place < owners)
+    owns = (rep >= first) & (rep < first + owners)
+    place = lax.rem(rep - first + owners * replicas, owners)
 
     def line_device(r, zz):
         return (r, device(y, x, zz, core)[1])

time: 38.4 us -> 38.4 us (level)
  no operation moved by 1% of the time
where the time goes in v5:
time: 38.4 us; the launch traced here: 38.2 us
  Pallas kernels  37.6 us (98%)
  between operations  0.64 us (2%)
    pallas_call x1, Pallas kernels, exchange(): pl.pallas_call(functools.partial(exchange_kernel, replicas), out_shape=(j...  35.5 us
    pallas_call x1, Pallas kernels, finish(): pl.pallas_call(functools.partial(finish_kernel, count), out_shape=shapes,...  2.13 us

profile of v5, /device:TPU:1, one launch (start us, length us, event | category | flops | bytes accessed | tf_op | source)
XLA Modules:
  0.0 38.2 jit_solution(17488482613871859085)
XLA Ops:
  0.6 35.5 %shard_map.128 = (f32[112,128]{1,0:T(8,128)}, f32[64,128]{1,0:T(8,128)}, f32[1,128]{1,0:T(1,128)}) custom-call(bf16[256,7168]{1,0:T(8,128)(2,1)} %tok_hbm.1, bf16[256,128]{1,0:T(8,128)(2,1)} %cot_hbm.1, s32[1,256]{1,0:T(1,128)} %bitcast.1, f32[1,8,4096]{2,1,0:T(8,128)} %loc_hbm.3, f32[8,4096]{1,0:T(8,128)} %glob_hbm.3, s32[8]{0:T(128)} %order_hbm.3), custom_call_target="tpu_custom_call" | custom-call | flops 469762048 | bytes 3670016 | tf_op jit(solution)/shard_map/pallas_call | solution.py:480
  36.1 2.1 %shard_map.129 = (f32[1,112,128]{2,1,0:T(8,128)}, f32[1,112]{1,0:T(1,128)}, f32[1,8,4096]{2,1,0:T(8,128)}, f32[8,4096]{1,0:T(8,128)}, f32[8,4096]{1,0:T(8,128)}) custom-call(s32[8]{0:T(128)} %order_hbm.3, f32[112,128]{1,0:T(8,128)} %get-tuple-element.8.sum_hbm, f32[64,128]{1,0:T(8,128)} %get-tuple-element.9.avg_hbm, f32[1,128]{1,0:T(1,128)} %get-tuple-element.10.sq_hbm, ...), custom_call_target="tpu_custom_call" | custom-call | tf_op jit(solution)/shard_map/pallas_call | solution.py:648
